TPU v7x, 512 devices: a whole 4x8x8 slice. The times are simulated.
512 devices in a mesh: row: 16 (over z, x_hi), col: 32 (over y, x_lo, core).
Axes of the slice: x: 4 (x_hi: 2, x_lo: 2; x = x_hi * 2 + x_lo), y: 8, z: 8, core: 2. Of those that a mesh axis runs over, the one named last changes fastest.
Arguments:
- hamiltonian: float32 [12288, 12288], P('row', 'col'), may hold values from -40 to 40, as said below
- panel: float32 [12288, 256], P('row'), may hold values from -180 to 180
Outputs:
- updated: float32 [12288, 12288], P('row', 'col')
- band_block: float32 [256, 256], replicated
Inputs may be any that keep to these rules, and one draw needn't show every extreme that they name: hamiltonian is exactly symmetric.
All inputs are finite; a program needn't handle non-finite values.
Results may differ from a plain program's by a relative error of at most 0.0003.
Values sent between devices are 32-bit elements; how exact they have to be, the bound alone decides.
A program may use at most 64 MiB of HBM per device.

v0:
```python
import jax
import jax.numpy as jnp
from jax import lax
from jax.sharding import PartitionSpec as P


def from_root(shard, axis, root):
    mine = lax.axis_index(axis) == root
    return lax.psum(jnp.where(mine, shard, jnp.zeros_like(shard)), axis)


def mult(left, right):
    return jnp.dot(left, right, precision=lax.Precision.HIGHEST, preferred_element_type=jnp.float32)


def lower_solve(low, rows):
    return jax.scipy.linalg.solve_triangular(low, rows.T, lower=True).T


def shards(hamiltonian, panel):
    rows_dev = panel.shape[0]
    width = panel.shape[1]
    cols_dev = hamiltonian.shape[1]
    row_place = lax.axis_index("row")
    col_place = lax.axis_index("col")
    global_rows = row_place * rows_dev + jnp.arange(rows_dev, dtype=jnp.int32)
    picker = (jnp.arange(width, dtype=jnp.int32)[:, None] == global_rows[None, :]).astype(
        jnp.float32
    )
    top_part = mult(picker, panel)
    gram, top_rows = lax.psum((mult(panel.T, panel), top_part), "row")
    first_low = jnp.linalg.cholesky(gram)
    half = lower_solve(first_low, panel)
    second_low = jnp.linalg.cholesky(lax.psum(mult(half.T, half), "row"))
    ortho = lower_solve(second_low, half)
    ortho_top = lower_solve(second_low, lower_solve(first_low, top_rows))
    ident = jnp.eye(width, dtype=jnp.float32)
    lead = ortho_top + ident
    factor = jax.scipy.linalg.cho_solve((jnp.linalg.cholesky(mult(lead, lead.T)), True), lead)
    reflectors = ortho + picker.T
    owner = col_place * cols_dev // rows_dev
    offset = col_place * cols_dev - owner * rows_dev
    reflect_slab = lax.dynamic_slice_in_dim(reflectors, offset, cols_dev, 0)
    reflect_cols = from_root(reflect_slab, "row", owner)
    partial_rows = mult(hamiltonian, reflect_cols)
    products = lax.psum(partial_rows, "col")
    images = mult(products, factor)
    coupling = lax.psum(mult(reflectors.T, images), "row")
    turned = mult(factor.T, coupling)
    correction = images - 0.5 * mult(reflectors, turned)
    correct_slab = lax.dynamic_slice_in_dim(correction, offset, cols_dev, 0)
    correct_cols = from_root(correct_slab, "row", owner)
    left_side = jnp.concatenate([reflectors, correction], axis=1)
    right_side = jnp.concatenate([correct_cols, reflect_cols], axis=1)
    updated = hamiltonian - mult(left_side, right_side.T)
    band_block = -mult(second_low.T, first_low.T)
    return (updated, band_block)


def solution(mesh):
    in_specs = (P("row", "col"), P("row", None))
    out_specs = (P("row", "col"), P())
    return jax.shard_map(shards, mesh=mesh, in_specs=in_specs, out_specs=out_specs, check_vma=False)
```

profile of v0, /device:TPU:1, one launch (start us, length us, event | category | flops | bytes accessed | tf_op | source)
XLA Modules:
  0.0 1277.8 jit_solution(7536185049286069226)
XLA Ops:
  7.2 3.5 fusion.78
  10.8 159.4 %all-reduce.9.cloned.1.call-done = f32[256,256]{0,1:T(8,128)} async-done(((f32[256,256]{0,1:T(8,128)}), f32[256,256]{0,1:T(8,128)}) %all-reduce.9.cloned.1.call-update) | async-done | bytes 262160 | tf_op jit(solution)/shard_map/psum | solution.py:31
  172.3 11.7 cholesky.172
  184.1 9.8 custom-call.24
  194.4 11.7 cholesky.189
  208.4 4.4 while.12
  212.7 19.7 %custom-call.25 = f32[2,128,128]{1,2,0:T(8,128)S(1)} custom-call(f32[2,128,128]{2,1,0:T(8,128)S(1)} %get-tuple-element.47), custom_call_target="InvertDiagBlocksLowerTriangular" | custom-call | tf_op jit(solution)/shard_map/jit(_solve_triangular)/triangular_solve | solution.py:17
  237.3 159.6 %all-reduce.11.cloned.1.call-done = f32[256,256]{0,1:T(8,128)} async-done(((f32[256,256]{0,1:T(8,128)}), f32[256,256]{0,1:T(8,128)}) %all-reduce.11.cloned.1.call-update) | async-done | bytes 262160 | tf_op jit(solution)/shard_map/psum | solution.py:34
  399.0 11.7 cholesky.206
  411.4 9.8 custom-call.26
  421.7 11.7 cholesky.223
  435.5 15.1 %while.13 = (s32[]{:T(128)}, f32[256,256]{1,0:T(8,128)S(1)}, s32[2,2]{1,0:T(2,128)S(1)}, f32[2,128,128]{2,1,0:T(8,128)S(1)}, s32[]{:T(128)}) while((s32[]{:T(128)}, f32[256,256]{1,0:T(8,128)S(1)}, s32[2,2]{1,0:T(2,128)S(1)}, f32[2,128,128]{2,1,0:T(8,128)S(1)}, s32[]{:T(128)}) %tuple.97), condition=%wide.while_cond.clone, body=%wide.while_body.clone.sunk | while | flops 2 | bytes 131189 | solution.py:17
  450.5 19.7 %custom-call.27 = f32[2,128,128]{1,2,0:T(8,128)S(1)} custom-call(f32[2,128,128]{2,1,0:T(8,128)S(1)} %get-tuple-element.48), custom_call_target="InvertDiagBlocksLowerTriangular" | custom-call | tf_op jit(solution)/shard_map/jit(_solve_triangular)/triangular_solve | solution.py:17
  472.7 162.9 %all-reduce.19.cloned.1.call-done = (f32[384,256]{0,1:T(8,128)}, f32[256,256]{0,1:T(8,128)}) async-done(((f32[384,256]{0,1:T(8,128)}, f32[256,256]{0,1:T(8,128)}), (f32[384,256]{0,1:T(8,128)}, f32[256,256]{0,1:T(8,128)})) %all-reduce.19.cloned.1.call-update) | async-done | bytes 655376 | tf_op jit(solution)/shard_map/psum | solution.py:9
  640.2 11.7 cholesky.240
  652.6 9.8 custom-call.30
  662.9 11.9 cholesky.257
  676.8 4.0 while.11
  680.9 19.7 %custom-call.18 = f32[2,128,128]{1,2,0:T(8,128)S(1)} custom-call(f32[2,128,128]{2,1,0:T(8,128)S(1)} %get-tuple-element.28), custom_call_target="InvertDiagBlocksLowerTriangular" | custom-call | tf_op jit(solution)/shard_map/jit(_cho_solve)/triangular_solve | solution.py:39
  701.3 2.3 convolution_bitcast_fusion
  704.9 237.8 %all-reduce.13.cloned.1.call-done = f32[768,256]{0,1:T(8,128)} async-done(((f32[768,256]{0,1:T(8,128)}), f32[768,256]{0,1:T(8,128)}) %all-reduce.13.cloned.1.call-update) | async-done | bytes 786448 | tf_op jit(solution)/shard_map/psum | solution.py:46
  946.5 154.0 %all-reduce.15.cloned.1.call-done = f32[256,256]{1,0:T(8,128)} async-done(((f32[256,256]{1,0:T(8,128)}), f32[256,256]{1,0:T(8,128)}) %all-reduce.15.cloned.1.call-update) | async-done | bytes 262160 | tf_op jit(solution)/shard_map/psum | solution.py:48
  1105.3 160.4 %all-reduce.17.cloned.1.call-done = f32[384,256]{0,1:T(8,128)} async-done(((f32[384,256]{0,1:T(8,128)}), f32[384,256]{0,1:T(8,128)}) %all-reduce.17.cloned.1.call-update) | async-done | bytes 393232 | tf_op jit(solution)/shard_map/psum | solution.py:9
  1265.7 4.8 fusion.4
  (112 shorter events, 43.5 us)
Async XLA Ops:
  7.2 163.1 %all-reduce.9.cloned.1.call-start = ((), (), s32[]{:S(2)}) async-start(), calls=%async_computation | async-start | bytes 524288 | tf_op jit(solution)/shard_map/psum | solution.py:31
  10.8 386.1 %all-reduce.11.cloned.1.call-start = ((), (), s32[]{:S(2)}) async-start(), calls=%async_computation.1 | async-start | bytes 524288 | tf_op jit(solution)/shard_map/psum | solution.py:34
  193.9 38.5 %copy-start = (f32[768,256]{1,0:T(8,128)S(1)}, f32[768,256]{1,0:T(8,128)}, u32[]{:S(2)}) copy-start(f32[768,256]{1,0:T(8,128)} %param.8) | copy-start | bytes 2359300
  206.2 26.2 %copy-start.2 = (f32[256,256]{1,0:T(8,128)}, f32[256,256]{1,0:T(8,128)S(1)}, u32[]{:S(2)}) copy-start(f32[256,256]{1,0:T(8,128)S(1)} %get-tuple-element.93) | copy-start | bytes 786436
  235.9 399.8 %all-reduce.19.cloned.1.call-start = ((), (), s32[]{:S(2)}) async-start(), calls=%async_computation.5 | async-start | bytes 1310720 | tf_op jit(solution)/shard_map/psum | solution.py:9
  433.4 37.3 %copy-start.4 = (f32[256,256]{1,0:T(8,128)}, f32[256,256]{1,0:T(8,128)S(1)}, u32[]{:S(2)}) copy-start(f32[256,256]{1,0:T(8,128)S(1)} %get-tuple-element.89) | copy-start | bytes 786436
  472.7 469.9 %all-reduce.13.cloned.1.call-start = ((), (), s32[]{:S(2)}) async-start(), calls=%async_computation.2 | async-start | bytes 1572864 | tf_op jit(solution)/shard_map/psum | solution.py:46
  674.8 26.4 %copy-start.1 = (f32[768,384]{1,0:T(8,128)S(1)}, f32[768,384]{1,0:T(8,128)}, u32[]{:S(2)}) copy-start(f32[768,384]{1,0:T(8,128)} %param.7) | copy-start | bytes 3538948
  674.8 26.4 %copy-start.6 = (f32[384,256]{0,1:T(8,128)S(1)}, f32[384,256]{0,1:T(8,128)}, u32[]{:S(2)}) copy-start(f32[384,256]{0,1:T(8,128)} %get-tuple-element.76) | copy-start | bytes 1179652
  703.6 396.8 %all-reduce.15.cloned.1.call-start = ((), (), s32[]{:S(2)}) async-start(), calls=%async_computation.3 | async-start | bytes 524288 | tf_op jit(solution)/shard_map/psum | solution.py:48
  946.2 319.5 %all-reduce.17.cloned.1.call-start = ((), (), s32[]{:S(2)}) async-start(), calls=%async_computation.4 | async-start | bytes 786432 | tf_op jit(solution)/shard_map/psum | solution.py:9
  1102.9 1.0 copy-start.3
  1102.9 1.2 copy-start.5
Sparse Core Ops, SparseCore 0:
  11.5 158.7 all-reduce.8
  236.0 160.8 all-reduce.10
  472.8 162.7 all-reduce.18
  703.8 238.8 all-reduce.12
  946.3 154.1 all-reduce.14
  1104.1 161.5 all-reduce.16
where the time goes:
time: 1300 us; the launch traced here: 1280 us
  waiting for transfers between devices  1030 us (79%)
  other arithmetic  166 us (13%)
  matrix products  31.5 us (2%)
  between operations  19 us (1%)
  local copies, waits for them, and re-layouts  14.7 us (1%)
    psum x2, waiting for transfers between devices, from_root(): return lax.psum(jnp.where(mine, shard, jnp.zeros_like(shard)), axis)  323 us
    psum x1, waiting for transfers between devices, shards(): products = lax.psum(partial_rows, 'col')  238 us
    psum x1, waiting for transfers between devices, shards(): second_low = jnp.linalg.cholesky(lax.psum(mult(half.T, half), 'row'))  160 us
    psum x1, waiting for transfers between devices, shards(): gram, top_rows = lax.psum((mult(panel.T, panel), top_part), 'row')  159 us
    psum x1, waiting for transfers between devices, shards(): coupling = lax.psum(mult(reflectors.T, images), 'row')  154 us
    another operation x5, other arithmetic, lower_solve(): return jax.scipy.linalg.solve_triangular(low, rows.T, lower=True).T  39.4 us
    another operation x7, other arithmetic, shards(): jnp.linalg.cholesky(mult(lead, lead.T))  34.8 us
    another operation x7, other arithmetic, shards(): second_low = jnp.linalg.cholesky(lax.psum(mult(half.T, half), 'row'))  34.6 us
  transfers between devices with their start and end apart: 6, of which 6 were waited for; matrix products, arithmetic and copies ran while one was open for 0% of the time, Pallas kernels for 0%

commit v1 on v0

v1 whole, which is shorter than its diff:
```python
import functools

import jax
import jax.numpy as jnp
from jax import lax
from jax.experimental import pallas as pl
from jax.experimental.pallas import tpu as pltpu
from jax.sharding import PartitionSpec as P

HI = lax.Precision.HIGHEST
MESH = pl.DeviceIdType.MESH
N = 256


def mm(a, b, ca, cb):
    return lax.dot_general(a, b, (((ca,), (cb,)), ((), ())), precision=HI, preferred_element_type=jnp.float32)

def spread(x, i, rows):
    return jnp.broadcast_to(x[i:i+1, :], (rows, 128))

def stack(parts):
    parts = [p for p in parts if p.shape[0]]
    return parts[0] if len(parts) == 1 else jnp.concatenate(parts, axis=0)

def halves(o):
    return ([0, 1] if o < 128 else [1]), ([0] if o < 128 else [0, 1])

def chol_inv(a, w, u, li, B):
    row = lax.broadcasted_iota(jnp.int32, (N, N), 0)
    col = lax.broadcasted_iota(jnp.int32, (N, N), 1)
    w[...] = jnp.where(row == col, 1.0, 0.0).astype(jnp.float32)
    sub = lax.broadcasted_iota(jnp.int32, (8, 128), 0)
    for o in range(0, N, B):
        ha, hw = halves(o)
        X = [a[o:o+B, 128*h:128*h+128] for h in ha] + [w[o:o+B, 128*h:128*h+128] for h in hw]
        for q in range(0, B, 8):
            k0 = o + q
            R = B - q
            base = X[ha.index(k0 // 128)]
            l0 = k0 % 128
            C = [jnp.broadcast_to(base[:, l0+k:l0+k+1], (R, 128)) for k in range(8)]
            scale = jnp.ones((8, 128), jnp.float32)
            for i in range(0, 8, 2):
                pa, pb, pd = C[i][i:i+1, :], C[i][i+1:i+2, :], C[i+1][i+1:i+2, :]
                pa, pb, pd = [jnp.broadcast_to(p, (8, 128)) for p in (pa, pb, pd)]
                det = pa*pd - pb*pb
                ra = 1.0 / pa
                rdet = 1.0 / det
                scale = jnp.where(sub == i, lax.rsqrt(pa), jnp.where(sub == i+1, lax.rsqrt(det*ra), scale))
                full = lambda p: jnp.concatenate([p]*(R//8), axis=0) if R > 8 else p
                fa, fb, fra, frd = full(pa), full(pb), full(ra), full(rdet)
                m2 = (C[i+1]*fa - C[i]*fb)*frd
                m1 = (C[i] - m2*fb)*fra
                m2 = stack([jnp.where(sub > i+1, m2[:8], 0.0), m2[8:]])
                m1 = stack([jnp.where(sub > i+1, m1[:8], jnp.where(sub == i+1, pb*ra, 0.0)), m1[8:]])
                for k in range(i+2, 8):
                    C[k] = (C[k] - m1*spread(C[k], i, R)) - m2*spread(C[k], i+1, R)
                X = [(x - m1*spread(x, i, R)) - m2*spread(x, i+1, R) for x in X]
            top = [x[:8]*scale for x in X]
            X = [x[8:] for x in X]
            for j, h in enumerate(ha):
                u[k0:k0+8, 128*h:128*h+128] = top[j]
            for j, h in enumerate(hw):
                li[k0:k0+8, 128*h:128*h+128] = top[len(ha)+j]
            if ha == [1]:
                u[k0:k0+8, 0:128] = jnp.zeros((8, 128), jnp.float32)
            if hw == [0]:
                li[k0:k0+8, 128:256] = jnp.zeros((8, 128), jnp.float32)
        e = o + B
        if e < N:
            a0 = 128 * (e // 128)
            lw = 128 if e <= 128 else 256
            for (m0, m1) in ((e, e+B), (e+B, N)):
                if m0 >= m1: continue
                lhs = u[o:e, :][:, m0:m1]
                a[m0:m1, a0:N] -= mm(lhs, u[o:e, a0:N], 0, 0)
                w[m0:m1, 0:lw] -= mm(lhs, li[o:e, 0:lw], 0, 0)
    u[...] = jnp.where(row <= col, u[...], 0.0)

def gj_init(w):
    row = lax.broadcasted_iota(jnp.int32, (N, N), 0)
    col = lax.broadcasted_iota(jnp.int32, (N, N), 1)
    w[...] = jnp.where(row == col, 1.0, 0.0).astype(jnp.float32)

def gj_inv(a, w, o, B):
    sub = lax.broadcasted_iota(jnp.int32, (8, 128), 0)
    ha, hw = halves(o)
    X = [a[o:o+B, 128*h:128*h+128] for h in ha] + [w[o:o+B, 128*h:128*h+128] for h in hw]
    scales = []
    for q in range(0, B, 8):
        k0 = o + q
        base = X[ha.index(k0 // 128)]
        l0 = k0 % 128
        C = [jnp.broadcast_to(base[:, l0+k:l0+k+1], (B, 128)) for k in range(8)]
        scale = jnp.ones((8, 128), jnp.float32)
        for i in range(8):
            p = jnp.broadcast_to(C[i][q+i:q+i+1, :], (8, 128))
            r = 1.0 / p
            scale = jnp.where(sub == i, r, scale)
            m = C[i] * (jnp.concatenate([r]*(B//8), axis=0) if B > 8 else r)
            m = stack([m[:q], jnp.where(sub == i, 0.0, m[q:q+8]), m[q+8:]])
            for k in range(i+1, 8):
                C[k] = C[k] - m*spread(C[k], q+i, B)
            X = [x - m*spread(x, q+i, B) for x in X]
        scales.append(scale)
    scale = jnp.concatenate(scales, axis=0)
    X = [x*scale for x in X]
    for j, h in enumerate(ha):
        a[o:o+B, 128*h:128*h+128] = X[j]
    for j, h in enumerate(hw):
        w[o:o+B, 128*h:128*h+128] = X[len(ha)+j]
    e = o + B
    a0 = 128 * (e // 128)
    lw = 128 if e <= 128 else 256
    h = o // 128
    for (m0, m1) in ((0, o), (e, N)):
        if m0 >= m1: continue
        lhs = a[m0:m1, 128*h:128*h+128][:, o-128*h:e-128*h]
        if a0 < N:
            a[m0:m1, a0:N] -= mm(lhs, a[o:e, a0:N], 1, 0)
        w[m0:m1, 0:lw] -= mm(lhs, w[o:e, 0:lw], 1, 0)

PHASES = ("g1", "g1c", "tr", "top", "pc", "topg", "g2", "g2c", "s", "sx", "sg", "hr", "hc", "hrg", "hcg",
          "m_g1", "m_g2", "m_top", "m_h0", "m_h1", "m_s", "m_sg", "m_hg")


def kernel(p_any, h_any, out_ref, band_ref, p_ref, hbuf, gp, ex1, ex2, g1, g2, pts, pt, pcs, pc,
           half, vr, vc, a, w, u1, l1, u2, l2, mbuf, mrecv, obuf, cbuf, crs, rrs, hvr, hvc,
           sbuf, srs, s1, smate, scx, sfull, p_sem, h_sem, send, recv):
    r = lax.axis_index("row")
    c = lax.axis_index("col")
    core = lax.rem(c, 2)
    chip = lax.div(c, 2)
    other = 1 - core
    mate = (r, 2 * chip + other)
    turned = (chip, 2 * r + core)
    diag = chip == r
    done = []

    def rcopy(src, dst, name, dev):
        i = PHASES.index(name)
        return pltpu.make_async_remote_copy(src_ref=src, dst_ref=dst, send_sem=send.at[i], recv_sem=recv.at[i],
                                            device_id=dev, device_id_type=MESH)

    def one(src, dst, name, dev):
        rcopy(src, dst, name, dev).start()
        done.append(lambda: rcopy(src, dst, name, dev).wait_send())

    def got(dst, name):
        rcopy(dst, dst, name, mate).wait_recv()

    def row_dev(k):
        return (k, c)

    def col_dev(k):
        return (r, 2 * k + core)

    def spread(name, me, dev, src, dst, fifteen):
        def step(d, x):
            k = lax.rem(me + d, 16)
            rcopy(src(k), dst, name, dev(k)).start()
            return x
        lax.fori_loop(1, 16, step, 0)
        done.append(lambda: rcopy(fifteen, fifteen, name, mate).wait_send())

    def rows(ref, k, n):
        return ref.at[pl.ds(pl.multiple_of(k * n, 8), n), :]

    def total(ref):
        t = ref[0]
        for k in range(1, 16):
            t = t + ref[k]
        return t

    p_copy = pltpu.make_async_copy(p_any, p_ref, p_sem)
    p_copy.start()
    h_copy = pltpu.make_async_copy(h_any, hbuf, h_sem)
    h_copy.start()

    barrier = pltpu.get_barrier_semaphore()

    def greet(d, x):
        pl.semaphore_signal(barrier, inc=1, device_id=row_dev(lax.rem(r + d, 16)), device_id_type=MESH)
        pl.semaphore_signal(barrier, inc=1, device_id=col_dev(lax.rem(chip + d, 16)), device_id_type=MESH)
        return x
    lax.fori_loop(1, 16, greet, 0)
    pl.semaphore_signal(barrier, inc=1, device_id=mate, device_id_type=MESH)

    @pl.when(jnp.logical_not(diag))
    def _():
        pl.semaphore_signal(barrier, inc=1, device_id=turned, device_id_type=MESH)

    my_cols = pl.ds(pl.multiple_of(core * 128, 128), 128)
    p_copy.wait()

    def gram_start(x_ref, name, ex):
        gp[...] = mm(x_ref[:, my_cols], x_ref[...], 0, 0)
        ex[r] = rows(gp, chip, 8)[...]

    def gram_send(name, ex):
        spread(name, r, row_dev, lambda k: ex.at[r], ex.at[r], ex.at[0:15])

    def gram_sum(name, ex, g):
        got(ex.at[0:15], name)
        mine = rows(g.at[core], chip, 8)
        mine[...] = total(ex)
        spread(name + "c", chip, col_dev, lambda k: mine, mine, g.at[0, 0:120])

    def gram_finish(name, g):
        got(g.at[0, 0:120], name + "c")
        one(g.at[core], g.at[core], "m_" + name, mate)

    def gram_place(name, g):
        got(g.at[other], "m_" + name)
        a[0:128, :] = g[0]
        a[128:256, :] = g[1]

    gram_start(p_ref, "g1", ex1)
    pl.semaphore_wait(barrier, 32 - diag.astype(jnp.int32))
    gram_send("g1", ex1)

    slab = pl.ds(pl.multiple_of(core * 384 + chip * 24, 8), 24)

    def piece():
        return rcopy(p_ref.at[slab, :], pcs, "tr", turned)

    def top(k):
        return rcopy(p_ref.at[pl.ds(pl.multiple_of(k * 16, 16), 16), my_cols], pts, "top", row_dev(k))

    @pl.when(diag)
    def _():
        pcs[...] = p_ref[slab, :]

    @pl.when(jnp.logical_not(diag))
    def _():
        piece().start()

    @pl.when(r == 0)
    def _():
        def step(k, x):
            top(k).start()
            return x
        lax.fori_loop(1, 16, step, 0)
        pts[...] = p_ref[0:16, my_cols]

    def scattered():
        @pl.when(jnp.logical_not(diag))
        def _():
            piece().wait_send()

        @pl.when(r == 0)
        def _():
            rcopy(p_ref.at[0:240, 0:128], p_ref.at[0:240, 0:128], "top", mate).wait_send()
    done.append(scattered)

    gram_sum("g1", ex1, g1)
    gram_finish("g1", g1)

    @pl.when(jnp.logical_not(diag))
    def _():
        piece().wait_recv()
    pc_mine = rows(pc, r, 24)
    pc_mine[...] = pcs[...]
    spread("pc", r, row_dev, lambda k: pcs, pc_mine, pc.at[0:360])
    gram_place("g1", g1)
    chol_inv(a, w, u1, l1, 64)

    half[...] = mm(p_ref[...], l1[...], 1, 1)
    gram_start(half, "g2", ex2)
    gram_send("g2", ex2)
    got(pc.at[0:360], "pc")
    vc[...] = mm(pc[...], l1[...], 1, 1)
    gram_sum("g2", ex2, g2)
    gram_finish("g2", g2)

    @pl.when(r != 0)
    def _():
        top(0).wait_recv()
    top_mine = rows(pt.at[core], r, 16)
    top_mine[...] = pts[...]
    spread("topg", r, row_dev, lambda k: pts, top_mine, pt.at[0, 0:240])
    gram_place("g2", g2)
    chol_inv(a, w, u2, l2, 64)

    grow = lax.broadcasted_iota(jnp.int32, (N, N), 0)
    gcol = lax.broadcasted_iota(jnp.int32, (N, N), 1)
    ident = jnp.where(grow == gcol, 1.0, 0.0).astype(jnp.float32)
    vc[...] = mm(vc[...], l2[...], 1, 1)

    @pl.when(c == 0)
    def _():
        vc[0:N, :] += ident
    h_copy.wait()

    theirs = pl.multiple_of(other * 384, 384)
    ours = pl.multiple_of(core * 384, 384)
    mbuf[...] = mm(hbuf[pl.ds(theirs, 384), :], vc[...], 1, 0)
    one(mbuf.at[0:192], mrecv.at[0:192], "m_h0", mate)
    one(mbuf.at[192:384], mrecv.at[192:384], "m_h1", mate)
    obuf[...] = mm(hbuf[pl.ds(ours, 384), :], vc[...], 1, 0)
    vr[...] = mm(half[...], l2[...], 1, 1)

    @pl.when(r == 0)
    def _():
        vr[0:N, :] += ident
    got(mrecv.at[0:192], "m_h0")
    obuf[0:192, :] += mrecv[0:192, :]
    got(mrecv.at[192:384], "m_h1")
    obuf[192:384, :] += mrecv[192:384, :]

    sv = mm(vr[pl.ds(ours, 384), :], obuf[...], 0, 0)
    sbuf[0] = sv[0:128, :]
    sbuf[1] = sv[128:256, :]

    def s_piece(k):
        return sbuf.at[:, pl.ds(pl.multiple_of(k * 8, 8), 8), :]
    srs[r] = s_piece(r)[...]
    spread("s", r, row_dev, s_piece, srs.at[r], srs.at[0:15])
    crs[chip] = rows(obuf, chip, 24)[...]
    spread("hr", chip, col_dev, lambda k: rows(obuf, k, 24), crs.at[chip], crs.at[0:15])
    cbuf[...] = mm(hbuf[...], vr[...], 0, 0)
    rrs[r] = rows(cbuf, r, 24)[...]
    spread("hc", r, row_dev, lambda k: rows(cbuf, k, 24), rrs.at[r], rrs.at[0:15])

    got(pt.at[0, 0:240], "topg")
    one(pt.at[core], pt.at[core], "m_top", mate)
    got(pt.at[other], "m_top")
    a[...] = mm(jnp.concatenate([pt[0], pt[1]], axis=1), l1[...], 1, 1)
    a[...] = mm(a[...], l2[...], 1, 1) + ident
    gj_init(w)
    gj_inv(a, w, 0, 32)
    gj_inv(a, w, 32, 32)
    gj_inv(a, w, 64, 32)

    got(srs.at[0:15], "s")
    s1[...] = total(srs)
    one(s1.at[other], smate, "m_s", mate)
    gj_inv(a, w, 96, 32)
    got(smate, "m_s")
    scx[chip] = s1[core] + smate[...]
    spread("sx", chip, col_dev, lambda k: scx.at[chip], scx.at[chip], scx.at[0:15])
    gj_inv(a, w, 128, 32)
    gj_inv(a, w, 160, 32)

    own = hvr.at[pl.ds(ours, 384), :]
    got(crs.at[0:15], "hr")
    hr_mine = rows(own, chip, 24)
    hr_mine[...] = total(crs)
    spread("hrg", chip, col_dev, lambda k: hr_mine, hr_mine, hvr.at[0:360])
    got(scx.at[0:15], "sx")
    s_mine = rows(sfull.at[core], r, 8)
    s_mine[...] = total(scx)
    spread("sg", r, row_dev, lambda k: s_mine, s_mine, sfull.at[0, 0:120])
    got(rrs.at[0:15], "hc")
    hc_mine = rows(hvc, r, 24)
    hc_mine[...] = total(rrs)
    spread("hcg", r, row_dev, lambda k: hc_mine, hc_mine, hvc.at[0:360])
    gj_inv(a, w, 192, 32)
    gj_inv(a, w, 224, 32)
    vr[...] = mm(vr[...], w[...], 1, 0)
    vc[...] = mm(vc[...], w[...], 1, 0)
    got(sfull.at[0, 0:120], "sg")
    one(sfull.at[core], sfull.at[core], "m_sg", mate)
    got(hvr.at[0:360], "hrg")
    one(own, own, "m_hg", mate)
    got(sfull.at[other], "m_sg")
    sv = mm(sfull[0], vc[...], 1, 1)
    sw = mm(sfull[1], vc[...], 1, 1)
    hbuf[...] += mm(vr[:, 0:128], sv, 1, 0) + mm(vr[:, 128:256], sw, 1, 0)
    got(hvr.at[pl.ds(theirs, 384), :], "m_hg")
    hbuf[...] -= mm(hvr[...], vc[...], 1, 1)
    got(hvc.at[0:360], "hcg")
    out_ref[...] = hbuf[...] - mm(vr[...], hvc[...], 1, 1)
    band_ref[...] = -mm(u2[...], u1[...], 1, 0)

    for f in done:
        f()


def shards(hamiltonian, panel):
    vm = pl.BlockSpec(memory_space=pltpu.VMEM)
    hbm = pl.BlockSpec(memory_space=pl.ANY)
    f32 = lambda *s: pltpu.VMEM(s, jnp.float32)
    sq = f32(N, N)
    two = f32(2, 128, N)
    scratch = [f32(768, N), f32(768, 384), f32(128, N), f32(16, 8, N), f32(16, 8, N), two, two,
               f32(16, 128), f32(2, N, 128), f32(24, N), f32(384, N),
               f32(768, N), f32(768, N), f32(384, N), sq, sq, sq, sq, sq, sq,
               f32(384, N), f32(384, N), f32(384, N), f32(384, N), f32(16, 24, N), f32(16, 24, N),
               f32(768, N), f32(384, N),
               two, f32(16, 2, 8, N), f32(2, 8, N), f32(8, N), f32(16, 8, N), two,
               pltpu.SemaphoreType.DMA, pltpu.SemaphoreType.DMA,
               pltpu.SemaphoreType.DMA((len(PHASES),)), pltpu.SemaphoreType.DMA((len(PHASES),))]
    return pl.pallas_call(
        kernel,
        out_shape=[jax.ShapeDtypeStruct((768, 384), jnp.float32), jax.ShapeDtypeStruct((N, N), jnp.float32)],
        in_specs=[hbm, hbm],
        out_specs=[vm, vm],
        scratch_shapes=scratch,
        compiler_params=pltpu.CompilerParams(collective_id=0, has_side_effects=True, vmem_limit_bytes=62 * 2**20),
        cost_estimate=pl.CostEstimate(flops=3 * 10**9, bytes_accessed=4 * 10**6, transcendentals=0),
    )(panel, hamiltonian)


def solution(mesh):
    in_specs = (P("row", "col"), P("row", None))
    out_specs = (P("row", "col"), P())
    return jax.shard_map(shards, mesh=mesh, in_specs=in_specs, out_specs=out_specs, check_vma=False)
```

time: 1300 us -> 110 us (0.08); the launches traced: 1280 us -> 110 us
  waiting for transfers between devices: 1030 us -> 0 us
  other arithmetic: 166 us -> 0 us
  Pallas kernels: 0 us -> 106 us
  matrix products: 31.5 us -> 0 us
  between operations: 19 us -> 0.65 us
    psum x6 -> x0, waiting for transfers between devices: 1030 us -> none  [the longest x2 323 us: from_root(): return lax.psum(jnp.where(mine, shard, jnp.zeros_like(shard)), axis)]
    another operation x27 -> x0, other arithmetic: 163 us -> none  [the longest x5 39.4 us: lower_solve(): return jax.scipy.linalg.solve_triangular(low, rows.T, lower=True).T]
    pallas_call x0 -> x1, Pallas kernels: none -> 106 us  [shards(): pl.pallas_call(kernel, out_shape=[jax.ShapeDtypeStruct((768, 384), jnp.fl...]
    dot_general x11 -> x0, matrix products: 21.2 us -> none  [mult(): jnp.dot(left, right, precision=lax.Precision.HIGHEST, preferred_element_t...]
  transfers between devices with their start and end apart: 6 -> 0, of which waited for: 6 -> 0; matrix products, arithmetic and copies ran while one was open for 0% -> 0% of each run, Pallas kernels for 0% -> 0%
where the time goes in v1:
time: 110 us
  Pallas kernels  106 us (96%)
  local copies, waits for them, and re-layouts  3.11 us (3%)
    pallas_call x1, Pallas kernels, shards(): pl.pallas_call(kernel, out_shape=[jax.ShapeDtypeStruct((768, 384), jnp.fl...  106 us
    unnamed x4, local copies, waits for them, and re-layouts  3.11 us

profile of v1, /device:TPU:1, one launch (start us, length us, event | category | flops | bytes accessed | tf_op | source)
XLA Modules:
  0.0 110.2 jit_solution(16647101094976430043)
XLA Ops:
  0.6 106.5 %shard_map.41 = (f32[768,384]{1,0:T(8,128)}, f32[256,256]{1,0:T(8,128)}) custom-call(f32[768,256]{1,0:T(8,128)} %p_any.1, f32[768,384]{1,0:T(8,128)} %h_any.1), custom_call_target="tpu_custom_call" | custom-call | flops 3000000000 | bytes 4000000 | tf_op jit(solution)/shard_map/pallas_call | solution.py:394
  107.1 0.0 copy-start
  107.1 2.4 %copy.6 = f32[768,384]{1,0:T(8,128)} copy(f32[768,384]{1,0:T(8,128)} %get-tuple-element.4) | data formatting | bytes 2359296
  109.5 0.0 copy-done
  109.5 0.7 copy.7
Async XLA Ops:
  107.1 2.4 %copy-start = (f32[256,256]{1,0:T(8,128)S(1)}, f32[256,256]{1,0:T(8,128)}, u32[]{:S(2)}) copy-start(f32[256,256]{1,0:T(8,128)} %get-tuple-element.5) | copy-start | bytes 786436

commit v2 on v1

--- a/solution.py
+++ b/solution.py
@@ -25,7 +25,7 @@
 def halves(o):
     return ([0, 1] if o < 128 else [1]), ([0] if o < 128 else [0, 1])
 
-def chol_inv(a, w, u, li, B):
+def chol_inv(a, w, u, li, B, after=()):
     row = lax.broadcasted_iota(jnp.int32, (N, N), 0)
     col = lax.broadcasted_iota(jnp.int32, (N, N), 1)
     w[...] = jnp.where(row == col, 1.0, 0.0).astype(jnp.float32)
@@ -67,6 +67,9 @@
             if hw == [0]:
                 li[k0:k0+8, 128:256] = jnp.zeros((8, 128), jnp.float32)
         e = o + B
+        for at, then in after:
+            if at == e:
+                then()
         if e < N:
             a0 = 128 * (e // 128)
             lw = 128 if e <= 128 else 256
@@ -121,12 +124,13 @@
         w[m0:m1, 0:lw] -= mm(lhs, w[o:e, 0:lw], 1, 0)
 
 PHASES = ("g1", "g1c", "tr", "top", "pc", "topg", "g2", "g2c", "s", "sx", "sg", "hr", "hc", "hrg", "hcg",
-          "m_g1", "m_g2", "m_top", "m_h0", "m_h1", "m_s", "m_sg", "m_hg")
+          "m_g1", "m_g2", "m_top", "m_h0", "m_h1", "m_s", "m_sg", "m_hg",
+          "he", "hea", "heb", "ht", "m_ht", "sb", "m_b", "sxb", "htx", "htg")
 
 
 def kernel(p_any, h_any, out_ref, band_ref, p_ref, hbuf, gp, ex1, ex2, g1, g2, pts, pt, pcs, pc,
-           half, vr, vc, a, w, u1, l1, u2, l2, mbuf, mrecv, obuf, cbuf, crs, rrs, hvr, hvc,
-           sbuf, srs, s1, smate, scx, sfull, p_sem, h_sem, send, recv):
+           half, vr, vc, a, w, u1, l1, u2, l2, mbuf, mrecv, obuf, crs, hha, hhb, hvr, hvc,
+           sbuf, srs, s1, smate, scx, sfull, bbuf, brs, b1, bmate, sxb, he, hea, heb, ht2, htt, htq, p_sem, h_sem, send, recv):
     r = lax.axis_index("row")
     c = lax.axis_index("col")
     core = lax.rem(c, 2)
@@ -142,12 +146,18 @@
         return pltpu.make_async_remote_copy(src_ref=src, dst_ref=dst, send_sem=send.at[i], recv_sem=recv.at[i],
                                             device_id=dev, device_id_type=MESH)
 
-    def one(src, dst, name, dev):
-        rcopy(src, dst, name, dev).start()
-        done.append(lambda: rcopy(src, dst, name, dev).wait_send())
-
-    def got(dst, name):
-        rcopy(dst, dst, name, mate).wait_recv()
+    def when(cond, f):
+        if cond is None:
+            f()
+        else:
+            pl.when(cond)(f)
+
+    def one(src, dst, name, dev, cond=None):
+        when(cond, lambda: rcopy(src, dst, name, dev).start())
+        done.append(lambda: when(cond, lambda: rcopy(src, dst, name, dev).wait_send()))
+
+    def got(dst, name, cond=None):
+        when(cond, lambda: rcopy(dst, dst, name, mate).wait_recv())
 
     def row_dev(k):
         return (k, c)
@@ -155,13 +165,13 @@
     def col_dev(k):
         return (r, 2 * k + core)
 
-    def spread(name, me, dev, src, dst, fifteen):
+    def spread(name, me, dev, src, dst, fifteen, cond=None):
         def step(d, x):
             k = lax.rem(me + d, 16)
             rcopy(src(k), dst, name, dev(k)).start()
             return x
-        lax.fori_loop(1, 16, step, 0)
-        done.append(lambda: rcopy(fifteen, fifteen, name, mate).wait_send())
+        when(cond, lambda: lax.fori_loop(1, 16, step, None))
+        done.append(lambda: when(cond, lambda: rcopy(fifteen, fifteen, name, mate).wait_send()))
 
     def rows(ref, k, n):
         return ref.at[pl.ds(pl.multiple_of(k * n, 8), n), :]
@@ -253,7 +263,42 @@
             rcopy(p_ref.at[0:240, 0:128], p_ref.at[0:240, 0:128], "top", mate).wait_send()
     done.append(scattered)
 
+    first, lead_chip = c == 0, chip == 0
+    h_copy.wait()
+
+    @pl.when(first)
+    def _():
+        he[...] = hbuf[0:384, 0:N]
+    ht_root = jnp.logical_and(first, r == 0)
+
+    @pl.when(ht_root)
+    def _():
+        ht2[0] = hbuf[0:8, 0:N]
+        ht2[1] = hbuf[128:136, 0:N]
+    one(hbuf.at[384:768, 0:N], he, "he", mate, first)
+    hbuf_sent = [done.pop()]
+
+    def ht_send(k, x):
+        for q in range(2):
+            rcopy(hbuf.at[pl.ds(pl.multiple_of(q * 128 + k * 8, 8), 8), 0:N], ht2.at[q], "ht", row_dev(k)).start()
+        return x
+    when(ht_root, lambda: lax.fori_loop(1, 16, ht_send, None))
+    hbuf_sent.append(lambda: when(ht_root, lambda: rcopy(hbuf.at[0:240, 0:N], hbuf.at[0:240, 0:N], "ht", mate).wait_send()))
+
     gram_sum("g1", ex1, g1)
+
+    @pl.when(r != 0)
+    def _():
+        top(0).wait_recv()
+    top_mine = rows(pt.at[core], r, 16)
+    top_mine[...] = pts[...]
+    spread("topg", r, row_dev, lambda k: pts, top_mine, pt.at[0, 0:240])
+    got(he, "he", c == 1)
+
+    @pl.when(lead_chip)
+    def _():
+        hea[...] = he[0:24, :]
+    spread("hea", chip, col_dev, lambda k: rows(he, k, 24), hea, he.at[0:360], lead_chip)
     gram_finish("g1", g1)
 
     @pl.when(jnp.logical_not(diag))
@@ -262,35 +307,34 @@
     pc_mine = rows(pc, r, 24)
     pc_mine[...] = pcs[...]
     spread("pc", r, row_dev, lambda k: pcs, pc_mine, pc.at[0:360])
+    got(hea, "hea", jnp.logical_not(lead_chip))
+
+    @pl.when(diag)
+    def _():
+        heb[...] = hea[...]
+    one(hea, heb, "heb", turned, jnp.logical_not(diag))
+    got(ht2, "ht", jnp.logical_and(first, r != 0))
+
+    @pl.when(first)
+    def _():
+        htt[...] = ht2[0]
+    one(ht2.at[1], htt, "m_ht", mate, first)
     gram_place("g1", g1)
-    chol_inv(a, w, u1, l1, 64)
+
+    def ht_cross():
+        got(htt, "m_ht", c == 1)
+
+        @pl.when(lead_chip)
+        def _():
+            htq[...] = htt[...]
+        spread("htx", chip, col_dev, lambda k: htt, htq, ex1.at[0:15], lead_chip)
+    chol_inv(a, w, u1, l1, 64, ((64, ht_cross),))
 
     half[...] = mm(p_ref[...], l1[...], 1, 1)
     gram_start(half, "g2", ex2)
     gram_send("g2", ex2)
     got(pc.at[0:360], "pc")
     vc[...] = mm(pc[...], l1[...], 1, 1)
-    gram_sum("g2", ex2, g2)
-    gram_finish("g2", g2)
-
-    @pl.when(r != 0)
-    def _():
-        top(0).wait_recv()
-    top_mine = rows(pt.at[core], r, 16)
-    top_mine[...] = pts[...]
-    spread("topg", r, row_dev, lambda k: pts, top_mine, pt.at[0, 0:240])
-    gram_place("g2", g2)
-    chol_inv(a, w, u2, l2, 64)
-
-    grow = lax.broadcasted_iota(jnp.int32, (N, N), 0)
-    gcol = lax.broadcasted_iota(jnp.int32, (N, N), 1)
-    ident = jnp.where(grow == gcol, 1.0, 0.0).astype(jnp.float32)
-    vc[...] = mm(vc[...], l2[...], 1, 1)
-
-    @pl.when(c == 0)
-    def _():
-        vc[0:N, :] += ident
-    h_copy.wait()
 
     theirs = pl.multiple_of(other * 384, 384)
     ours = pl.multiple_of(core * 384, 384)
@@ -298,80 +342,123 @@
     one(mbuf.at[0:192], mrecv.at[0:192], "m_h0", mate)
     one(mbuf.at[192:384], mrecv.at[192:384], "m_h1", mate)
     obuf[...] = mm(hbuf[pl.ds(ours, 384), :], vc[...], 1, 0)
-    vr[...] = mm(half[...], l2[...], 1, 1)
-
-    @pl.when(r == 0)
-    def _():
-        vr[0:N, :] += ident
     got(mrecv.at[0:192], "m_h0")
     obuf[0:192, :] += mrecv[0:192, :]
     got(mrecv.at[192:384], "m_h1")
     obuf[192:384, :] += mrecv[192:384, :]
 
-    sv = mm(vr[pl.ds(ours, 384), :], obuf[...], 0, 0)
+    sv = mm(half[pl.ds(ours, 384), :], obuf[...], 0, 0)
     sbuf[0] = sv[0:128, :]
     sbuf[1] = sv[128:256, :]
-
-    def s_piece(k):
-        return sbuf.at[:, pl.ds(pl.multiple_of(k * 8, 8), 8), :]
-    srs[r] = s_piece(r)[...]
-    spread("s", r, row_dev, s_piece, srs.at[r], srs.at[0:15])
+    one(sbuf.at[other], smate, "m_s", mate)
+
+    @pl.when(lead_chip)
+    def _():
+        bv = mm(half[pl.ds(ours, 384), :], he[...], 0, 0)
+        bbuf[0] = bv[0:128, :]
+        bbuf[1] = bv[128:256, :]
+    one(bbuf.at[other], bmate, "m_b", mate, lead_chip)
+    got(smate, "m_s")
+    s1[...] = sbuf[core] + smate[...]
+    srs[r] = rows(s1, r, 8)[...]
+    spread("s", r, row_dev, lambda k: rows(s1, k, 8), srs.at[r], srs.at[0:15])
+    got(bmate, "m_b", lead_chip)
+
+    @pl.when(lead_chip)
+    def _():
+        b1[...] = bbuf[core] + bmate[...]
+        brs[r] = rows(b1, r, 8)[...]
+    spread("sb", r, row_dev, lambda k: rows(b1, k, 8), brs.at[r], brs.at[0:15], lead_chip)
+    gram_sum("g2", ex2, g2)
     crs[chip] = rows(obuf, chip, 24)[...]
     spread("hr", chip, col_dev, lambda k: rows(obuf, k, 24), crs.at[chip], crs.at[0:15])
-    cbuf[...] = mm(hbuf[...], vr[...], 0, 0)
-    rrs[r] = rows(cbuf, r, 24)[...]
-    spread("hc", r, row_dev, lambda k: rows(cbuf, k, 24), rrs.at[r], rrs.at[0:15])
-
-    got(pt.at[0, 0:240], "topg")
-    one(pt.at[core], pt.at[core], "m_top", mate)
+    s_early = sfull.at[core, 2, pl.ds(pl.multiple_of(r * 8, 8), 8), :]
+    got(htq, "htx", jnp.logical_not(lead_chip))
+    s_early[...] = htq[...]
+    spread("htg", r, row_dev, lambda k: htq, s_early, sfull.at[0, 2, 0:120])
+    gram_finish("g2", g2)
+    gram_place("g2", g2)
+
+    def s_cross():
+        got(srs.at[0:15], "s")
+        scx[chip] = total(srs)
+        spread("sx", chip, col_dev, lambda k: scx.at[chip], scx.at[chip], scx.at[0:15])
+        got(brs.at[0:15], "sb", lead_chip)
+
+        @pl.when(lead_chip)
+        def _():
+            sxb[...] = total(brs)
+        spread("sxb", chip, col_dev, lambda k: sxb, sxb, scx.at[0:15], lead_chip)
+
+    def turn():
+        got(crs.at[0:15], "hr")
+        hha[...] = total(crs)
+
+        @pl.when(diag)
+        def _():
+            hhb[...] = hha[...]
+        one(hha, hhb, "hc", turned, jnp.logical_not(diag))
+
+    def top_share():
+        got(pt.at[0, 0:240], "topg")
+        one(pt.at[core], pt.at[core], "m_top", mate)
+    chol_inv(a, w, u2, l2, 64, ((64, s_cross), (128, top_share), (192, turn)))
+
+    grow = lax.broadcasted_iota(jnp.int32, (N, N), 0)
+    gcol = lax.broadcasted_iota(jnp.int32, (N, N), 1)
+    ident = jnp.where(grow == gcol, 1.0, 0.0).astype(jnp.float32)
+    own = hvr.at[pl.ds(ours, 384), :]
+    got(scx.at[0:15], "sx")
+    got(sxb, "sxb", jnp.logical_not(lead_chip))
+    s_mine = sfull.at[core, 0:2, pl.ds(pl.multiple_of(r * 8, 8), 8), :]
+    s_mine[0] = total(scx)
+    s_mine[1] = sxb[...]
+    spread("sg", r, row_dev, lambda k: s_mine, s_mine, sfull.at[0, 0:2, 0:120])
+    hr_mine = rows(own, chip, 24)
+    hr_mine[...] = mm(hha[...], l2[...], 1, 1) + hea[...]
+    spread("hrg", chip, col_dev, lambda k: hr_mine, hr_mine, hvr.at[0:360])
+    vr[...] = mm(half[...], l2[...], 1, 1)
+    vc[...] = mm(vc[...], l2[...], 1, 1)
+
+    @pl.when(r == 0)
+    def _():
+        vr[0:N, :] += ident
+
+    @pl.when(c == 0)
+    def _():
+        vc[0:N, :] += ident
+
     got(pt.at[other], "m_top")
     a[...] = mm(jnp.concatenate([pt[0], pt[1]], axis=1), l1[...], 1, 1)
     a[...] = mm(a[...], l2[...], 1, 1) + ident
     gj_init(w)
     gj_inv(a, w, 0, 32)
-    gj_inv(a, w, 32, 32)
-    gj_inv(a, w, 64, 32)
-
-    got(srs.at[0:15], "s")
-    s1[...] = total(srs)
-    one(s1.at[other], smate, "m_s", mate)
-    gj_inv(a, w, 96, 32)
-    got(smate, "m_s")
-    scx[chip] = s1[core] + smate[...]
-    spread("sx", chip, col_dev, lambda k: scx.at[chip], scx.at[chip], scx.at[0:15])
-    gj_inv(a, w, 128, 32)
-    gj_inv(a, w, 160, 32)
-
-    own = hvr.at[pl.ds(ours, 384), :]
-    got(crs.at[0:15], "hr")
-    hr_mine = rows(own, chip, 24)
-    hr_mine[...] = total(crs)
-    spread("hrg", chip, col_dev, lambda k: hr_mine, hr_mine, hvr.at[0:360])
-    got(scx.at[0:15], "sx")
-    s_mine = rows(sfull.at[core], r, 8)
-    s_mine[...] = total(scx)
-    spread("sg", r, row_dev, lambda k: s_mine, s_mine, sfull.at[0, 0:120])
-    got(rrs.at[0:15], "hc")
+    got(hhb, "hc", jnp.logical_not(diag))
+    got(heb, "heb", jnp.logical_not(diag))
     hc_mine = rows(hvc, r, 24)
-    hc_mine[...] = total(rrs)
+    hc_mine[...] = mm(hhb[...], l2[...], 1, 1) + heb[...]
     spread("hcg", r, row_dev, lambda k: hc_mine, hc_mine, hvc.at[0:360])
-    gj_inv(a, w, 192, 32)
-    gj_inv(a, w, 224, 32)
+    for o in range(32, N, 32):
+        gj_inv(a, w, o, 32)
     vr[...] = mm(vr[...], w[...], 1, 0)
     vc[...] = mm(vc[...], w[...], 1, 0)
-    got(sfull.at[0, 0:120], "sg")
+
+    band_ref[...] = -mm(u2[...], u1[...], 1, 0)
+    got(sfull.at[0, 2, 0:120], "htg")
+    got(sfull.at[0, 0:2, 0:120], "sg")
     one(sfull.at[core], sfull.at[core], "m_sg", mate)
+    got(sfull.at[other], "m_sg")
+    shh, sb, stt = [jnp.concatenate([sfull[0, i], sfull[1, i]], axis=0) for i in range(3)]
+    a[...] = mm(mm(l2[...], shh, 1, 0), l2[...], 1, 1) + mm(l2[...], sb, 1, 0) + mm(sb, l2[...], 0, 1) + stt
+    for f in hbuf_sent:
+        f()
+    hbuf[...] += mm(vr[...], mm(a[...], vc[...], 1, 1), 1, 0)
     got(hvr.at[0:360], "hrg")
     one(own, own, "m_hg", mate)
-    got(sfull.at[other], "m_sg")
-    sv = mm(sfull[0], vc[...], 1, 1)
-    sw = mm(sfull[1], vc[...], 1, 1)
-    hbuf[...] += mm(vr[:, 0:128], sv, 1, 0) + mm(vr[:, 128:256], sw, 1, 0)
     got(hvr.at[pl.ds(theirs, 384), :], "m_hg")
     hbuf[...] -= mm(hvr[...], vc[...], 1, 1)
     got(hvc.at[0:360], "hcg")
     out_ref[...] = hbuf[...] - mm(vr[...], hvc[...], 1, 1)
-    band_ref[...] = -mm(u2[...], u1[...], 1, 0)
 
     for f in done:
         f()
@@ -379,16 +466,18 @@
 
 def shards(hamiltonian, panel):
     vm = pl.BlockSpec(memory_space=pltpu.VMEM)
-    hbm = pl.BlockSpec(memory_space=pl.ANY)
+    hbm = pl.BlockSpec(memory_space=pltpu.HBM)
     f32 = lambda *s: pltpu.VMEM(s, jnp.float32)
     sq = f32(N, N)
     two = f32(2, 128, N)
     scratch = [f32(768, N), f32(768, 384), f32(128, N), f32(16, 8, N), f32(16, 8, N), two, two,
                f32(16, 128), f32(2, N, 128), f32(24, N), f32(384, N),
                f32(768, N), f32(768, N), f32(384, N), sq, sq, sq, sq, sq, sq,
-               f32(384, N), f32(384, N), f32(384, N), f32(384, N), f32(16, 24, N), f32(16, 24, N),
+               f32(384, N), f32(384, N), f32(384, N), f32(16, 24, N), f32(24, N), f32(24, N),
                f32(768, N), f32(384, N),
-               two, f32(16, 2, 8, N), f32(2, 8, N), f32(8, N), f32(16, 8, N), two,
+               two, f32(16, 8, N), f32(128, N), f32(128, N), f32(16, 8, N), f32(2, 3, 128, N),
+               two, f32(16, 8, N), f32(128, N), f32(128, N), f32(8, N), f32(384, N), f32(24, N), f32(24, N),
+               f32(2, 8, N), f32(8, N), f32(8, N),
                pltpu.SemaphoreType.DMA, pltpu.SemaphoreType.DMA,
                pltpu.SemaphoreType.DMA((len(PHASES),)), pltpu.SemaphoreType.DMA((len(PHASES),))]
     return pl.pallas_call(
@@ -397,7 +486,7 @@
         in_specs=[hbm, hbm],
         out_specs=[vm, vm],
         scratch_shapes=scratch,
-        compiler_params=pltpu.CompilerParams(collective_id=0, has_side_effects=True, vmem_limit_bytes=62 * 2**20),
+        compiler_params=pltpu.CompilerParams(collective_id=0, has_side_effects=True, vmem_limit_bytes=58 * 2**20),
         cost_estimate=pl.CostEstimate(flops=3 * 10**9, bytes_accessed=4 * 10**6, transcendentals=0),
     )(panel, hamiltonian)
 

time: 110 us -> 98.1 us (0.89); the launches traced: 110 us -> 97.2 us
  Pallas kernels: 106 us -> 93.4 us
    pallas_call x1, Pallas kernels: 106 us -> 93.4 us  [shards(): pl.pallas_call(kernel, out_shape=[jax.ShapeDtypeStruct((768, 384), jnp.fl...]
where the time goes in v2:
time: 98.1 us; the launch traced here: 97.2 us
  Pallas kernels  93.4 us (95%)
  local copies, waits for them, and re-layouts  3.11 us (3%)
    pallas_call x1, Pallas kernels, shards(): pl.pallas_call(kernel, out_shape=[jax.ShapeDtypeStruct((768, 384), jnp.fl...  93.4 us
    unnamed x4, local copies, waits for them, and re-layouts  3.11 us

profile of v2, /device:TPU:1, one launch (start us, length us, event | category | flops | bytes accessed | tf_op | source)
XLA Modules:
  0.0 97.2 jit_solution(4254294131515718021)
XLA Ops:
  0.6 93.4 %shard_map.41 = (f32[768,384]{1,0:T(8,128)}, f32[256,256]{1,0:T(8,128)}) custom-call(f32[768,256]{1,0:T(8,128)} %p_any.1, f32[768,384]{1,0:T(8,128)} %h_any.1), custom_call_target="tpu_custom_call" | custom-call | flops 3000000000 | bytes 4000000 | tf_op jit(solution)/shard_map/pallas_call | solution.py:483
  94.1 0.0 copy-start
  94.1 2.4 %copy.6 = f32[768,384]{1,0:T(8,128)} copy(f32[768,384]{1,0:T(8,128)} %get-tuple-element.4) | data formatting | bytes 2359296
  96.5 0.0 copy-done
  96.5 0.7 copy.7
Async XLA Ops:
  94.1 2.4 %copy-start = (f32[256,256]{1,0:T(8,128)S(1)}, f32[256,256]{1,0:T(8,128)}, u32[]{:S(2)}) copy-start(f32[256,256]{1,0:T(8,128)} %get-tuple-element.5) | copy-start | bytes 786436

commit v3 on v2

--- a/solution.py
+++ b/solution.py
@@ -417,17 +417,6 @@
     hr_mine = rows(own, chip, 24)
     hr_mine[...] = mm(hha[...], l2[...], 1, 1) + hea[...]
     spread("hrg", chip, col_dev, lambda k: hr_mine, hr_mine, hvr.at[0:360])
-    vr[...] = mm(half[...], l2[...], 1, 1)
-    vc[...] = mm(vc[...], l2[...], 1, 1)
-
-    @pl.when(r == 0)
-    def _():
-        vr[0:N, :] += ident
-
-    @pl.when(c == 0)
-    def _():
-        vc[0:N, :] += ident
-
     got(pt.at[other], "m_top")
     a[...] = mm(jnp.concatenate([pt[0], pt[1]], axis=1), l1[...], 1, 1)
     a[...] = mm(a[...], l2[...], 1, 1) + ident
@@ -440,8 +429,17 @@
     spread("hcg", r, row_dev, lambda k: hc_mine, hc_mine, hvc.at[0:360])
     for o in range(32, N, 32):
         gj_inv(a, w, o, 32)
-    vr[...] = mm(vr[...], w[...], 1, 0)
-    vc[...] = mm(vc[...], w[...], 1, 0)
+    a[...] = mm(l2[...], w[...], 0, 0)
+    vr[...] = mm(half[...], a[...], 1, 0)
+    vc[...] = mm(vc[...], a[...], 1, 0)
+
+    @pl.when(r == 0)
+    def _():
+        vr[0:N, :] += w[...]
+
+    @pl.when(c == 0)
+    def _():
+        vc[0:N, :] += w[...]
 
     band_ref[...] = -mm(u2[...], u1[...], 1, 0)
     got(sfull.at[0, 2, 0:120], "htg")

time: 98.1 us -> 97.7 us (level)
  no operation moved by 1% of the time
where the time goes in v3:
time: 97.7 us; the launch traced here: 96.8 us
  Pallas kernels  93 us (95%)
  local copies, waits for them, and re-layouts  3.11 us (3%)
    pallas_call x1, Pallas kernels, shards(): pl.pallas_call(kernel, out_shape=[jax.ShapeDtypeStruct((768, 384), jnp.fl...  93 us
    unnamed x4, local copies, waits for them, and re-layouts  3.11 us

profile of v3, /device:TPU:1, one launch (start us, length us, event | category | flops | bytes accessed | tf_op | source)
XLA Modules:
  0.0 96.8 jit_solution(6784647428019156060)
XLA Ops:
  0.6 93.0 %shard_map.41 = (f32[768,384]{1,0:T(8,128)}, f32[256,256]{1,0:T(8,128)}) custom-call(f32[768,256]{1,0:T(8,128)} %p_any.1, f32[768,384]{1,0:T(8,128)} %h_any.1), custom_call_target="tpu_custom_call" | custom-call | flops 3000000000 | bytes 4000000 | tf_op jit(solution)/shard_map/pallas_call | solution.py:481
  93.7 0.0 copy-start
  93.7 2.4 %copy.6 = f32[768,384]{1,0:T(8,128)} copy(f32[768,384]{1,0:T(8,128)} %get-tuple-element.4) | data formatting | bytes 2359296
  96.1 0.0 copy-done
  96.1 0.7 copy.7
Async XLA Ops:
  93.7 2.4 %copy-start = (f32[256,256]{1,0:T(8,128)S(1)}, f32[256,256]{1,0:T(8,128)}, u32[]{:S(2)}) copy-start(f32[256,256]{1,0:T(8,128)} %get-tuple-element.5) | copy-start | bytes 786436
